TPU v7x, 32 devices: a whole 2x2x4 slice. The times are simulated.
32 devices in a mesh: gx: 4 (over z), gy: 2 (over y), gz: 4 (over x, core).
Axes of the slice: x: 2, y: 2, z: 4, core: 2. Of those that a mesh axis runs over, the one named last changes fastest.
Arguments:
- velocity: float32 [3, 32, 16, 512], P(None, 'gx', 'gy', 'gz'), may hold values from -4 to 4
- sketch_prev: float32 [3, 16, 4, 32, 8, 128], P(None, 'gy', 'gz', 'gx'), may hold values from -6 to 6
- seed_matrix: int32 [512, 128], replicated, may hold values from -4 to 4
- snap_steps: int32 [4], replicated, may hold values from 0 to 511
- rank_keep: int32 [1], replicated, may hold values from 32 to 128
Outputs:
- velocity_out: float32 [3, 32, 16, 512], P(None, 'gx', 'gy', 'gz')
- mode_rows: float32 [3, 16, 4, 32, 8, 128], P(None, 'gy', 'gz', 'gx')
- factor: float32 [128, 128], replicated
All inputs are finite; a program needn't handle non-finite values.
Results may differ from a plain program's by a relative error of at most 0.0003.
Values sent between devices are 32-bit elements; how exact they have to be, the bound alone decides.
A program may use at most 64 MiB of HBM per device.

v0:
```python
import math

import jax
import jax.numpy as jnp
from jax import lax
from jax.sharding import PartitionSpec as P

SNAPS = 4
STEPS = 2


TIME_STEP = 0.1
VISCOSITY = 0.4
ONE_THIRD = 1.0 / 3.0
TWO_THIRDS = 2.0 / 3.0
HIGHEST = lax.Precision.HIGHEST


def extended(block, sides, width):
    for axis, dim in sides:
        count = lax.axis_size(axis)
        forward = [(i, i + 1) for i in range(count - 1)]
        forward.append((count - 1, 0))
        backward = [(target, source) for source, target in forward]
        low = lax.ppermute(
            lax.slice_in_dim(block, block.shape[dim] - width, None, axis=dim), axis, forward
        )
        high = lax.ppermute(lax.slice_in_dim(block, 0, width, axis=dim), axis, backward)
        block = jnp.concatenate([low, block, high], axis=dim)
    return block


def tendency(padded):
    center = padded[:, 1:-1, 1:-1, 1:-1]
    forward = (padded[:, 2:, 1:-1, 1:-1], padded[:, 1:-1, 2:, 1:-1], padded[:, 1:-1, 1:-1, 2:])
    backward = (padded[:, :-2, 1:-1, 1:-1], padded[:, 1:-1, :-2, 1:-1], padded[:, 1:-1, 1:-1, :-2])
    convect = (
        center[0:1] * (forward[0] - backward[0])
        + center[1:2] * (forward[1] - backward[1])
        + center[2:3] * (forward[2] - backward[2])
    )
    spread = (
        forward[0]
        + backward[0]
        + forward[1]
        + backward[1]
        + forward[2]
        + backward[2]
        - 6.0 * center
    )
    return -0.5 * convect + VISCOSITY * spread


def with_walls(padded, margin):
    cells_y = padded.shape[2] - 2 * margin
    wall_rows = (
        lax.axis_index("gy") * cells_y - margin + jnp.arange(cells_y + 2 * margin, dtype=jnp.int32)
    )
    inside = ((wall_rows >= 0) & (wall_rows < lax.axis_size("gy") * cells_y)).astype(jnp.float32)
    return padded * inside[None, None, :, None]


def faces_padded(current):
    return with_walls(extended(current, (("gx", 1), ("gy", 2), ("gz", 3)), 1), 1)


def step_by_section(current):
    first_section = current + TIME_STEP * tendency(faces_padded(current))
    second_section = 0.75 * current + 0.25 * (
        first_section + TIME_STEP * tendency(faces_padded(first_section))
    )
    return ONE_THIRD * current + TWO_THIRDS * (
        second_section + TIME_STEP * tendency(faces_padded(second_section))
    )


def coarse_local(current):
    cells_x = current.shape[1]
    cells_y = current.shape[2]
    cells_z = current.shape[3]
    blocks = current.reshape(3, cells_x // 4, 4, cells_y, cells_z // 4, 4)
    return jnp.transpose(jnp.mean(blocks, axis=(2, 5)), (0, 2, 3, 1))


def on_device(velocity, sketch_prev, seed_matrix, snap_steps, rank_keep):
    current = velocity
    collected = []
    for snap_index in range(SNAPS):
        for step_index in range(STEPS):
            current = step_by_section(current)
        local_snap = coarse_local(current)
        collected.append(lax.all_to_all(local_snap, "gx", split_axis=2, concat_axis=3, tiled=True))
    stacked = jnp.stack(collected)
    rank_total = sketch_prev.shape[-1]
    snap_rows = stacked.reshape(stacked.shape[0], -1)
    picker = (
        snap_steps[:, None] == jnp.arange(seed_matrix.shape[0], dtype=jnp.int32)[None, :]
    ).astype(jnp.float32)
    omega_rows = 0.5 * jnp.dot(picker, seed_matrix.astype(jnp.float32), precision=HIGHEST)
    sketch_rows = sketch_prev.reshape(-1, rank_total) + lax.dot_general(
        snap_rows, omega_rows, (((0,), (0,)), ((), ())), precision=HIGHEST
    )
    local_gram = lax.dot_general(
        sketch_rows, sketch_rows, (((0,), (0,)), ((), ())), precision=HIGHEST
    )
    gram_sum = lax.psum(local_gram, ("gx", "gy", "gz"))
    lower_factor = jnp.linalg.cholesky(gram_sum)
    identity = jnp.eye(rank_total, dtype=jnp.float32)
    inverse = lax.linalg.triangular_solve(lower_factor, identity, left_side=True, lower=True).T
    total_rows = (
        sketch_rows.shape[0] * lax.axis_size("gx") * lax.axis_size("gy") * lax.axis_size("gz")
    )
    norm_scale = math.sqrt(total_rows)
    inside = (jnp.arange(rank_total, dtype=jnp.int32) < rank_keep[0]).astype(jnp.float32)
    mode_rows = norm_scale * jnp.dot(sketch_rows, inverse, precision=HIGHEST) * inside[None, :]
    factor = lower_factor.T * (1.0 / norm_scale) * inside[:, None] * inside[None, :]
    return (current, mode_rows.reshape(sketch_prev.shape), factor)


def solution(mesh):
    placed = (P(None, "gx", "gy", "gz"), P(None, "gy", "gz", "gx", None, None), P(), P(), P())
    return jax.shard_map(
        on_device,
        mesh=mesh,
        in_specs=placed,
        out_specs=(P(None, "gx", "gy", "gz"), P(None, "gy", "gz", "gx", None, None), P()),
        check_vma=False,
    )
```

profile of v0, /device:TPU:0, one launch (start us, length us, event | category | flops | bytes accessed | tf_op | source)
XLA Modules:
  0.0 673.7 jit_solution(11360867830438096656)
XLA Ops:
  23.1 4.6 collective-permute-done.4
  29.9 3.4 collective-permute-start.7
  41.3 4.3 collective-permute-done.10
  48.3 3.5 collective-permute-start.13
  60.7 4.3 collective-permute-done.16
  79.5 3.9 collective-permute-done.22
  99.0 3.9 collective-permute-done.28
  118.4 3.9 collective-permute-done.34
  138.0 3.9 collective-permute-done.40
  157.0 3.9 collective-permute-done.46
  176.5 3.6 collective-permute-done.52
  195.9 3.9 collective-permute-done.58
  215.0 3.9 collective-permute-done.64
  234.5 3.9 collective-permute-done.70
  253.1 3.9 collective-permute-done.76
  273.0 3.9 collective-permute-done.82
  291.5 3.9 collective-permute-done.88
  311.5 3.9 collective-permute-done.94
  329.9 3.9 collective-permute-done.100
  337.7 12.8 %collective-permute-start.103 = (f32[3,1,8,128]{3,2,1,0:T(8,128)S(1)}, f32[3,1,8,128]{3,2,1,0:T(8,128)S(1)}, u32[]{:S(2)}, u32[]{:S(2)}) collective-permute-start(f32[3,1,8,128]{3,2,1,0:T(8,128)S(1)} %get-tuple-element.196), channel_id=1, source_target_pairs={{8,0},{16,8},{24,16},{0,24},{9,1},{17,9},{25,17},{1,25},{10,2},{18... | collective-permute-start | bytes 36872 | tf_op jit(solution)/shard_map/ppermute | solution.py:28
  359.4 3.9 collective-permute-done.106
  378.1 3.9 collective-permute-done.112
  397.9 3.9 collective-permute-done.118
  416.5 3.9 collective-permute-done.124
  436.3 3.9 collective-permute-done.130
  466.4 3.2 all-to-all-start
  484.5 5.1 all-to-all-start.1
  490.8 4.4 all-to-all-done.1
  499.3 4.7 all-to-all-done.2
  519.4 119.7 %all-reduce.2.cloned.1.call-done = f32[128,128]{0,1:T(8,128)} async-done(((f32[128,128]{0,1:T(8,128)}), f32[128,128]{0,1:T(8,128)}) %all-reduce.2.cloned.1.call-update) | async-done | bytes 65552 | tf_op jit(solution)/shard_map/psum | solution.py:106
  640.9 11.7 %cholesky.17 = f32[128,128]{1,0:T(8,128)S(1)} custom-call(f32[128,128]{1,0:T(8,128)S(1)} %fusion.155), custom_call_target="Cholesky" | custom-call | tf_op jit(solution)/shard_map/jit(cholesky)/cholesky | solution.py:107
  654.7 9.8 %custom-call.6 = f32[1,128,128]{1,2,0:T(8,128)S(1)} custom-call(f32[1,128,128]{2,1,0:T(8,128)S(1)} %get-tuple-element.232), custom_call_target="InvertDiagBlocksLowerTriangular" | custom-call | tf_op jit(solution)/shard_map/triangular_solve | solution.py:109
  (502 shorter events, 391.8 us)
Async XLA Ops:
  39.5 7.6 %collective-permute-start.11 = (f32[3,10,10,1]{3,2,1,0:T(8,128)S(1)}, f32[3,10,10,1]{3,2,1,0:T(8,128)S(1)}, u32[]{:S(2)}, u32[]{:S(2)}) collective-permute-start(f32[3,10,10,1]{3,2,1,0:T(8,128)S(1)} %get-tuple-element.132), channel_id=1, source_target_pairs={{1,0},{2,1},{3,2},{0,3},{5,4},{6,5},{7,6},{4,7},{9,8},{10,9},{11,1... | collective-permute-start | bytes 3608 | tf_op jit(solution)/shard_map/ppermute | solution.py:28
  58.9 7.6 %collective-permute-start.17 = (f32[3,10,10,1]{3,2,1,0:T(8,128)S(1)}, f32[3,10,10,1]{3,2,1,0:T(8,128)S(1)}, u32[]{:S(2)}, u32[]{:S(2)}) collective-permute-start(f32[3,10,10,1]{3,2,1,0:T(8,128)S(1)} %get-tuple-element.130), channel_id=1, source_target_pairs={{1,0},{2,1},{3,2},{0,3},{5,4},{6,5},{7,6},{4,7},{9,8},{10,9},{11,1... | collective-permute-start | bytes 3608 | tf_op jit(solution)/shard_map/ppermute | solution.py:28
  77.7 8.0 %collective-permute-start.23 = (f32[3,10,10,1]{3,2,1,0:T(8,128)S(1)}, f32[3,10,10,1]{3,2,1,0:T(8,128)S(1)}, u32[]{:S(2)}, u32[]{:S(2)}) collective-permute-start(f32[3,10,10,1]{3,2,1,0:T(8,128)S(1)} %get-tuple-element.128), channel_id=1, source_target_pairs={{1,0},{2,1},{3,2},{0,3},{5,4},{6,5},{7,6},{4,7},{9,8},{10,9},{11,1... | collective-permute-start | bytes 3608 | tf_op jit(solution)/shard_map/ppermute | solution.py:28
  97.3 8.1 %collective-permute-start.29 = (f32[3,10,10,1]{3,2,1,0:T(8,128)S(1)}, f32[3,10,10,1]{3,2,1,0:T(8,128)S(1)}, u32[]{:S(2)}, u32[]{:S(2)}) collective-permute-start(f32[3,10,10,1]{3,2,1,0:T(8,128)S(1)} %get-tuple-element.126), channel_id=1, source_target_pairs={{1,0},{2,1},{3,2},{0,3},{5,4},{6,5},{7,6},{4,7},{9,8},{10,9},{11,1... | collective-permute-start | bytes 3608 | tf_op jit(solution)/shard_map/ppermute | solution.py:28
  116.6 7.9 %collective-permute-start.35 = (f32[3,10,10,1]{3,2,1,0:T(8,128)S(1)}, f32[3,10,10,1]{3,2,1,0:T(8,128)S(1)}, u32[]{:S(2)}, u32[]{:S(2)}) collective-permute-start(f32[3,10,10,1]{3,2,1,0:T(8,128)S(1)} %get-tuple-element.124), channel_id=1, source_target_pairs={{1,0},{2,1},{3,2},{0,3},{5,4},{6,5},{7,6},{4,7},{9,8},{10,9},{11,1... | collective-permute-start | bytes 3608 | tf_op jit(solution)/shard_map/ppermute | solution.py:28
  136.2 7.8 %collective-permute-start.41 = (f32[3,10,10,1]{3,2,1,0:T(8,128)S(1)}, f32[3,10,10,1]{3,2,1,0:T(8,128)S(1)}, u32[]{:S(2)}, u32[]{:S(2)}) collective-permute-start(f32[3,10,10,1]{3,2,1,0:T(8,128)S(1)} %get-tuple-element.122), channel_id=1, source_target_pairs={{1,0},{2,1},{3,2},{0,3},{5,4},{6,5},{7,6},{4,7},{9,8},{10,9},{11,1... | collective-permute-start | bytes 3608 | tf_op jit(solution)/shard_map/ppermute | solution.py:28
  155.2 7.8 %collective-permute-start.47 = (f32[3,10,10,1]{3,2,1,0:T(8,128)S(1)}, f32[3,10,10,1]{3,2,1,0:T(8,128)S(1)}, u32[]{:S(2)}, u32[]{:S(2)}) collective-permute-start(f32[3,10,10,1]{3,2,1,0:T(8,128)S(1)} %get-tuple-element.120), channel_id=1, source_target_pairs={{1,0},{2,1},{3,2},{0,3},{5,4},{6,5},{7,6},{4,7},{9,8},{10,9},{11,1... | collective-permute-start | bytes 3608 | tf_op jit(solution)/shard_map/ppermute | solution.py:28
  174.6 8.0 %collective-permute-start.53 = (f32[3,10,10,1]{3,2,1,0:T(8,128)S(1)}, f32[3,10,10,1]{3,2,1,0:T(8,128)S(1)}, u32[]{:S(2)}, u32[]{:S(2)}) collective-permute-start(f32[3,10,10,1]{3,2,1,0:T(8,128)S(1)} %get-tuple-element.118), channel_id=1, source_target_pairs={{1,0},{2,1},{3,2},{0,3},{5,4},{6,5},{7,6},{4,7},{9,8},{10,9},{11,1... | collective-permute-start | bytes 3608 | tf_op jit(solution)/shard_map/ppermute | solution.py:28
  194.2 7.9 %collective-permute-start.59 = (f32[3,10,10,1]{3,2,1,0:T(8,128)S(1)}, f32[3,10,10,1]{3,2,1,0:T(8,128)S(1)}, u32[]{:S(2)}, u32[]{:S(2)}) collective-permute-start(f32[3,10,10,1]{3,2,1,0:T(8,128)S(1)} %get-tuple-element.116), channel_id=1, source_target_pairs={{1,0},{2,1},{3,2},{0,3},{5,4},{6,5},{7,6},{4,7},{9,8},{10,9},{11,1... | collective-permute-start | bytes 3608 | tf_op jit(solution)/shard_map/ppermute | solution.py:28
  213.2 7.6 %collective-permute-start.65 = (f32[3,10,10,1]{3,2,1,0:T(8,128)S(1)}, f32[3,10,10,1]{3,2,1,0:T(8,128)S(1)}, u32[]{:S(2)}, u32[]{:S(2)}) collective-permute-start(f32[3,10,10,1]{3,2,1,0:T(8,128)S(1)} %get-tuple-element.114), channel_id=1, source_target_pairs={{1,0},{2,1},{3,2},{0,3},{5,4},{6,5},{7,6},{4,7},{9,8},{10,9},{11,1... | collective-permute-start | bytes 3608 | tf_op jit(solution)/shard_map/ppermute | solution.py:28
  232.8 7.8 %collective-permute-start.71 = (f32[3,10,10,1]{3,2,1,0:T(8,128)S(1)}, f32[3,10,10,1]{3,2,1,0:T(8,128)S(1)}, u32[]{:S(2)}, u32[]{:S(2)}) collective-permute-start(f32[3,10,10,1]{3,2,1,0:T(8,128)S(1)} %get-tuple-element.112), channel_id=1, source_target_pairs={{1,0},{2,1},{3,2},{0,3},{5,4},{6,5},{7,6},{4,7},{9,8},{10,9},{11,1... | collective-permute-start | bytes 3608 | tf_op jit(solution)/shard_map/ppermute | solution.py:28
  251.4 7.5 %collective-permute-start.77 = (f32[3,10,10,1]{3,2,1,0:T(8,128)S(1)}, f32[3,10,10,1]{3,2,1,0:T(8,128)S(1)}, u32[]{:S(2)}, u32[]{:S(2)}) collective-permute-start(f32[3,10,10,1]{3,2,1,0:T(8,128)S(1)} %get-tuple-element.110), channel_id=1, source_target_pairs={{1,0},{2,1},{3,2},{0,3},{5,4},{6,5},{7,6},{4,7},{9,8},{10,9},{11,1... | collective-permute-start | bytes 3608 | tf_op jit(solution)/shard_map/ppermute | solution.py:28
  271.3 7.8 %collective-permute-start.83 = (f32[3,10,10,1]{3,2,1,0:T(8,128)S(1)}, f32[3,10,10,1]{3,2,1,0:T(8,128)S(1)}, u32[]{:S(2)}, u32[]{:S(2)}) collective-permute-start(f32[3,10,10,1]{3,2,1,0:T(8,128)S(1)} %get-tuple-element.108), channel_id=1, source_target_pairs={{1,0},{2,1},{3,2},{0,3},{5,4},{6,5},{7,6},{4,7},{9,8},{10,9},{11,1... | collective-permute-start | bytes 3608 | tf_op jit(solution)/shard_map/ppermute | solution.py:28
  289.8 7.5 %collective-permute-start.89 = (f32[3,10,10,1]{3,2,1,0:T(8,128)S(1)}, f32[3,10,10,1]{3,2,1,0:T(8,128)S(1)}, u32[]{:S(2)}, u32[]{:S(2)}) collective-permute-start(f32[3,10,10,1]{3,2,1,0:T(8,128)S(1)} %get-tuple-element.106), channel_id=1, source_target_pairs={{1,0},{2,1},{3,2},{0,3},{5,4},{6,5},{7,6},{4,7},{9,8},{10,9},{11,1... | collective-permute-start | bytes 3608 | tf_op jit(solution)/shard_map/ppermute | solution.py:28
  309.8 7.8 %collective-permute-start.95 = (f32[3,10,10,1]{3,2,1,0:T(8,128)S(1)}, f32[3,10,10,1]{3,2,1,0:T(8,128)S(1)}, u32[]{:S(2)}, u32[]{:S(2)}) collective-permute-start(f32[3,10,10,1]{3,2,1,0:T(8,128)S(1)} %get-tuple-element.104), channel_id=1, source_target_pairs={{1,0},{2,1},{3,2},{0,3},{5,4},{6,5},{7,6},{4,7},{9,8},{10,9},{11,1... | collective-permute-start | bytes 3608 | tf_op jit(solution)/shard_map/ppermute | solution.py:28
  328.2 7.6 %collective-permute-start.101 = (f32[3,10,10,1]{3,2,1,0:T(8,128)S(1)}, f32[3,10,10,1]{3,2,1,0:T(8,128)S(1)}, u32[]{:S(2)}, u32[]{:S(2)}) collective-permute-start(f32[3,10,10,1]{3,2,1,0:T(8,128)S(1)} %get-tuple-element.102), channel_id=1, source_target_pairs={{1,0},{2,1},{3,2},{0,3},{5,4},{6,5},{7,6},{4,7},{9,8},{10,9},{11,1... | collective-permute-start | bytes 3608 | tf_op jit(solution)/shard_map/ppermute | solution.py:28
  336.5 14.0 %collective-permute-start.102 = (f32[3,1,8,128]{3,2,1,0:T(8,128)S(1)}, f32[3,1,8,128]{3,2,1,0:T(8,128)S(1)}, u32[]{:S(2)}, u32[]{:S(2)}) collective-permute-start(f32[3,1,8,128]{3,2,1,0:T(8,128)S(1)} %get-tuple-element.195), channel_id=1, source_target_pairs={{0,8},{8,16},{16,24},{24,0},{1,9},{9,17},{17,25},{25,1},{2,10},{10... | collective-permute-start | bytes 36872 | tf_op jit(solution)/shard_map/ppermute | solution.py:25
  337.7 14.2 %collective-permute-start.103 = (f32[3,1,8,128]{3,2,1,0:T(8,128)S(1)}, f32[3,1,8,128]{3,2,1,0:T(8,128)S(1)}, u32[]{:S(2)}, u32[]{:S(2)}) collective-permute-start(f32[3,1,8,128]{3,2,1,0:T(8,128)S(1)} %get-tuple-element.196), channel_id=1, source_target_pairs={{8,0},{16,8},{24,16},{0,24},{9,1},{17,9},{25,17},{1,25},{10,2},{18... | collective-permute-start | bytes 36872 | tf_op jit(solution)/shard_map/ppermute | solution.py:28
  357.6 7.5 %collective-permute-start.107 = (f32[3,10,10,1]{3,2,1,0:T(8,128)S(1)}, f32[3,10,10,1]{3,2,1,0:T(8,128)S(1)}, u32[]{:S(2)}, u32[]{:S(2)}) collective-permute-start(f32[3,10,10,1]{3,2,1,0:T(8,128)S(1)} %get-tuple-element.100), channel_id=1, source_target_pairs={{1,0},{2,1},{3,2},{0,3},{5,4},{6,5},{7,6},{4,7},{9,8},{10,9},{11,1... | collective-permute-start | bytes 3608 | tf_op jit(solution)/shard_map/ppermute | solution.py:28
  376.4 7.5 %collective-permute-start.113 = (f32[3,10,10,1]{3,2,1,0:T(8,128)S(1)}, f32[3,10,10,1]{3,2,1,0:T(8,128)S(1)}, u32[]{:S(2)}, u32[]{:S(2)}) collective-permute-start(f32[3,10,10,1]{3,2,1,0:T(8,128)S(1)} %get-tuple-element.98), channel_id=1, source_target_pairs={{1,0},{2,1},{3,2},{0,3},{5,4},{6,5},{7,6},{4,7},{9,8},{10,9},{11,1... | collective-permute-start | bytes 3608 | tf_op jit(solution)/shard_map/ppermute | solution.py:28
  396.2 7.5 %collective-permute-start.119 = (f32[3,10,10,1]{3,2,1,0:T(8,128)S(1)}, f32[3,10,10,1]{3,2,1,0:T(8,128)S(1)}, u32[]{:S(2)}, u32[]{:S(2)}) collective-permute-start(f32[3,10,10,1]{3,2,1,0:T(8,128)S(1)} %get-tuple-element.96), channel_id=1, source_target_pairs={{1,0},{2,1},{3,2},{0,3},{5,4},{6,5},{7,6},{4,7},{9,8},{10,9},{11,1... | collective-permute-start | bytes 3608 | tf_op jit(solution)/shard_map/ppermute | solution.py:28
  414.7 7.5 %collective-permute-start.125 = (f32[3,10,10,1]{3,2,1,0:T(8,128)S(1)}, f32[3,10,10,1]{3,2,1,0:T(8,128)S(1)}, u32[]{:S(2)}, u32[]{:S(2)}) collective-permute-start(f32[3,10,10,1]{3,2,1,0:T(8,128)S(1)} %get-tuple-element.94), channel_id=1, source_target_pairs={{1,0},{2,1},{3,2},{0,3},{5,4},{6,5},{7,6},{4,7},{9,8},{10,9},{11,1... | collective-permute-start | bytes 3608 | tf_op jit(solution)/shard_map/ppermute | solution.py:28
  434.6 7.5 %collective-permute-start.131 = (f32[3,10,10,1]{3,2,1,0:T(8,128)S(1)}, f32[3,10,10,1]{3,2,1,0:T(8,128)S(1)}, u32[]{:S(2)}, u32[]{:S(2)}) collective-permute-start(f32[3,10,10,1]{3,2,1,0:T(8,128)S(1)} %get-tuple-element.92), channel_id=1, source_target_pairs={{1,0},{2,1},{3,2},{0,3},{5,4},{6,5},{7,6},{4,7},{9,8},{10,9},{11,1... | collective-permute-start | bytes 3608 | tf_op jit(solution)/shard_map/ppermute | solution.py:28
  453.1 7.5 %collective-permute-start.137 = (f32[3,10,10,1]{3,2,1,0:T(8,128)S(1)}, f32[3,10,10,1]{3,2,1,0:T(8,128)S(1)}, u32[]{:S(2)}, u32[]{:S(2)}) collective-permute-start(f32[3,10,10,1]{3,2,1,0:T(8,128)S(1)} %get-tuple-element.90), channel_id=1, source_target_pairs={{1,0},{2,1},{3,2},{0,3},{5,4},{6,5},{7,6},{4,7},{9,8},{10,9},{11,1... | collective-permute-start | bytes 3608 | tf_op jit(solution)/shard_map/ppermute | solution.py:28
  461.4 9.3 %collective-permute-start.138 = (f32[3,1,8,128]{3,2,1,0:T(8,128)S(1)}, f32[3,1,8,128]{3,2,1,0:T(8,128)S(1)}, u32[]{:S(2)}, u32[]{:S(2)}) collective-permute-start(f32[3,1,8,128]{3,2,1,0:T(8,128)S(1)} %get-tuple-element.183), channel_id=1, source_target_pairs={{0,8},{8,16},{16,24},{24,0},{1,9},{9,17},{17,25},{25,1},{2,10},{10... | collective-permute-start | bytes 36872 | tf_op jit(solution)/shard_map/ppermute | solution.py:25
  462.7 8.0 %collective-permute-start.139 = (f32[3,1,8,128]{3,2,1,0:T(8,128)S(1)}, f32[3,1,8,128]{3,2,1,0:T(8,128)S(1)}, u32[]{:S(2)}, u32[]{:S(2)}) collective-permute-start(f32[3,1,8,128]{3,2,1,0:T(8,128)S(1)} %get-tuple-element.184), channel_id=1, source_target_pairs={{8,0},{16,8},{24,16},{0,24},{9,1},{17,9},{25,17},{1,25},{10,2},{18... | collective-permute-start | bytes 36872 | tf_op jit(solution)/shard_map/ppermute | solution.py:28
  466.4 18.0 %all-to-all-start = ((f32[4,1,384]{2,1,0:T(1,128)}), f32[4,1,384]{2,1,0:T(1,128)S(1)}, u32[]{:S(2)}, u32[]{:S(2)}) async-start(f32[4,1,384]{2,1,0:T(1,128)} %reshape.77), calls=%async_computation | async-start | bytes 12288 | tf_op jit(solution)/shard_map/all_to_all | solution.py:92
  476.4 7.5 %collective-permute-start.143 = (f32[3,10,10,1]{3,2,1,0:T(8,128)S(1)}, f32[3,10,10,1]{3,2,1,0:T(8,128)S(1)}, u32[]{:S(2)}, u32[]{:S(2)}) collective-permute-start(f32[3,10,10,1]{3,2,1,0:T(8,128)S(1)} %get-tuple-element.88), channel_id=1, source_target_pairs={{1,0},{2,1},{3,2},{0,3},{5,4},{6,5},{7,6},{4,7},{9,8},{10,9},{11,1... | collective-permute-start | bytes 3608 | tf_op jit(solution)/shard_map/ppermute | solution.py:28
  484.5 10.7 %all-to-all-start.1 = ((f32[4,1,384]{2,1,0:T(1,128)}), f32[4,1,384]{2,1,0:T(1,128)S(1)}, u32[]{:S(2)}, u32[]{:S(2)}) async-start(f32[4,1,384]{2,1,0:T(1,128)} %reshape.75), calls=%async_computation.1 | async-start | bytes 12288 | tf_op jit(solution)/shard_map/all_to_all | solution.py:92
  495.1 8.8 %all-to-all-start.2 = ((f32[4,1,384]{2,1,0:T(1,128)}), f32[4,1,384]{2,1,0:T(1,128)S(1)}, u32[]{:S(2)}, u32[]{:S(2)}) async-start(f32[4,1,384]{2,1,0:T(1,128)} %reshape.73), calls=%async_computation.2 | async-start | bytes 12288 | tf_op jit(solution)/shard_map/all_to_all | solution.py:92
  504.0 9.9 %all-to-all-start.3 = ((f32[4,1,384]{2,1,0:T(1,128)}), f32[4,1,384]{2,1,0:T(1,128)S(1)}, u32[]{:S(2)}, u32[]{:S(2)}) async-start(f32[4,1,384]{2,1,0:T(1,128)} %reshape.71), calls=%async_computation.3 | async-start | bytes 12288 | tf_op jit(solution)/shard_map/all_to_all | solution.py:92
  507.2 131.8 %all-reduce.2.cloned.1.call-start = ((), (), s32[]{:S(2)}) async-start(), calls=%async_computation.4 | async-start | bytes 131072 | tf_op jit(solution)/shard_map/psum | solution.py:106
  (122 other events, 614.3 us)
Sparse Core Ops, SparseCore 0:
  519.5 119.5 all-reduce.1
where the time goes:
time: 684 us; the launch traced here: 674 us
  waiting for transfers between devices  370 us (54%)
  starting transfers between devices  217 us (32%)
  other arithmetic  45.2 us (7%)
  local copies, waits for them, and re-layouts  19.4 us (3%)
  between operations  16.8 us (2%)
    ppermute x72, waiting for transfers between devices, extended(): lax.ppermute(lax.slice_in_dim(block, block.shape[dim] - width, None, axis...  167 us
    ppermute x72, starting transfers between devices, extended(): lax.ppermute(lax.slice_in_dim(block, 0, width, axis=dim), axis, backward)  144 us
    psum x1, waiting for transfers between devices, on_device(): gram_sum = lax.psum(local_gram, ('gx', 'gy', 'gz'))  120 us
    ppermute x72, waiting for transfers between devices, extended(): lax.ppermute(lax.slice_in_dim(block, 0, width, axis=dim), axis, backward)  74 us
    ppermute x72, starting transfers between devices, extended(): lax.ppermute(lax.slice_in_dim(block, block.shape[dim] - width, None, axis...  57.3 us
    all_to_all x4, starting transfers between devices, on_device(): lax.all_to_all(local_snap, 'gx', split_axis=2, concat_axis=3, tiled=True)  14.8 us
  transfers between devices with their start and end apart: 149, of which 121 were waited for; matrix products, arithmetic and copies ran while one was open for 2% of the time, Pallas kernels for 0%

commit v1 on v0

--- a/solution.py
+++ b/solution.py
@@ -1,9 +1,15 @@
+import functools
 import math
 
 import jax
 import jax.numpy as jnp
 from jax import lax
+from jax.experimental import pallas as pl
+from jax.experimental.pallas import tpu as pltpu
 from jax.sharding import PartitionSpec as P
+
+MESH = pl.DeviceIdType.MESH
+VMEM_SPEC = pl.BlockSpec(memory_space=pltpu.VMEM)
 
 SNAPS = 4
 STEPS = 2
@@ -82,7 +88,381 @@
     return jnp.transpose(jnp.mean(blocks, axis=(2, 5)), (0, 2, 3, 1))
 
 
-def on_device(velocity, sketch_prev, seed_matrix, snap_steps, rank_keep):
+GROUP = 8
+CHUNK = 16
+HALO = 24
+REACH = (-2, -1, 0, 1, 2)
+
+
+def place_of(n):
+    m = n % GROUP
+    return (m // 2, m % 2, n // GROUP)
+
+
+def swap_groups(rows):
+    rows = list(rows)
+    lane = lax.broadcasted_iota(jnp.int32, rows[0].shape, 1)
+    for step in (1, 2, 4):
+        low = (lane // (CHUNK * step)) % 2 == 0
+        for i in range(GROUP):
+            if i & step:
+                continue
+            first, second = rows[i], rows[i | step]
+            rows[i] = jnp.where(low, first, pltpu.roll(second, CHUNK * step, 1))
+            rows[i | step] = jnp.where(low, pltpu.roll(first, 128 - CHUNK * step, 1), second)
+    return rows
+
+
+def meet(places):
+    barrier = pltpu.get_barrier_semaphore()
+    for place in places:
+        pl.semaphore_signal(barrier, inc=1, device_id=place, device_id_type=MESH)
+    pl.semaphore_wait(barrier, len(places))
+
+
+def gather_kernel(ring, v_ref, ext_ref, packed, send_a, recv_a, send_b, recv_b):
+    gx, gy, gz = lax.axis_index("gx"), lax.axis_index("gy"), lax.axis_index("gz")
+    m = 2 * gx + gy
+    n = GROUP * gz + m
+    mates = [((m + j) % GROUP) for j in range(1, GROUP)]
+    mate_places = [(k // 2, k % 2, gz) for k in mates]
+    offsets = [d for d in REACH if d != 0]
+    ring_places = [place_of((n + d + ring) % ring) for d in offsets]
+    rows = swap_groups([v_ref[:, x].reshape(24, 128) for x in range(8)])
+    for k in range(GROUP):
+        packed[k] = rows[k].reshape(3, 8, 128)
+    meet(mate_places + ring_places)
+    copies = []
+    for j in range(1, GROUP):
+        copy = pltpu.make_async_remote_copy(
+            src_ref=packed.at[mates[j - 1]],
+            dst_ref=ext_ref.at[2, m],
+            send_sem=send_a.at[j - 1],
+            recv_sem=recv_a.at[j - 1],
+            device_id=mate_places[j - 1],
+            device_id_type=MESH,
+        )
+        copy.start()
+        copies.append(copy)
+    ext_ref[2, m] = packed[m]
+    for copy in copies:
+        copy.wait()
+    copies = []
+    for i, d in enumerate(offsets):
+        copy = pltpu.make_async_remote_copy(
+            src_ref=ext_ref.at[2],
+            dst_ref=ext_ref.at[2 - d],
+            send_sem=send_b.at[i],
+            recv_sem=recv_b.at[i],
+            device_id=ring_places[i],
+            device_id_type=MESH,
+        )
+        copy.start()
+        copies.append(copy)
+    for copy in copies:
+        copy.wait()
+
+
+def gather_blocks(velocity, ring):
+    return pl.pallas_call(
+        functools.partial(gather_kernel, ring),
+        out_shape=jax.ShapeDtypeStruct((5, GROUP, 3, 8, 128), jnp.float32),
+        in_specs=[VMEM_SPEC],
+        out_specs=VMEM_SPEC,
+        scratch_shapes=[
+            pltpu.VMEM((GROUP, 3, 8, 128), jnp.float32),
+            pltpu.SemaphoreType.DMA((GROUP - 1,)),
+            pltpu.SemaphoreType.DMA((GROUP - 1,)),
+            pltpu.SemaphoreType.DMA((4,)),
+            pltpu.SemaphoreType.DMA((4,)),
+        ],
+        compiler_params=pltpu.CompilerParams(
+            collective_id=0, has_side_effects=True, vmem_limit_bytes=16 * 2**20
+        ),
+        name="gather_blocks",
+    )(velocity)
+
+
+def wrap_rows(buf):
+    buf[:, 0] = pltpu.roll(buf[:, 16].reshape(48, 128), 64, 1).reshape(3, 16, 128)
+    buf[:, 17] = pltpu.roll(buf[:, 1].reshape(48, 128), 64, 1).reshape(3, 16, 128)
+
+
+def section(src, base, dst, base_weight, weight):
+    row = lax.broadcasted_iota(jnp.int32, (16, 128), 0)
+    top, bottom = row == 15, row == 0
+    even = weight * TIME_STEP * VISCOSITY
+    odd = weight * TIME_STEP * 0.5
+    own = weight * (1.0 - 6.0 * TIME_STEP * VISCOSITY)
+
+    def one_row(r, carry):
+        center = [src[c, r] for c in range(3)]
+        ahead = [even - odd * center[j] for j in range(3)]
+        behind = [2.0 * even - ahead[j] for j in range(3)]
+        ahead[1] = jnp.where(top, 0.0, ahead[1])
+        behind[1] = jnp.where(bottom, 0.0, behind[1])
+        for c in range(3):
+            value = own * center[c]
+            x_part = ahead[0] * src[c, r + 1] + behind[0] * src[c, r - 1]
+            y_part = ahead[1] * pltpu.roll(center[c], 15, 0) + behind[1] * pltpu.roll(center[c], 1, 0)
+            z_part = ahead[2] * pltpu.roll(center[c], 127, 1) + behind[2] * pltpu.roll(center[c], 1, 1)
+            if base is not None:
+                value = value + base_weight * base[c, r]
+            dst[c, r] = (value + x_part) + (y_part + z_part)
+        return carry
+
+    lax.fori_loop(1, 17, one_row, 0, unroll=4)
+    wrap_rows(dst)
+
+
+def solve_kernel(ext_ref, back_ref, coarse_ref, v, a, b):
+    lane = lax.broadcasted_iota(jnp.int32, (24, 128), 1)
+    for far in range(2):
+        for y_half in range(2):
+            for x in range(8):
+                value = None
+                for half in range(2):
+                    for d in REACH:
+                        piece = ext_ref[d + 2, 2 * (2 * half + far) + y_half].reshape(24, 128)
+                        start = 64 * half + HALO + CHUNK * d
+                        piece = pltpu.roll(piece, (start - CHUNK * x) % 128, 1)
+                        if value is None:
+                            value = piece
+                        else:
+                            first = max(start, 64 * half)
+                            value = jnp.where(lane >= first, piece, value)
+                v[:, 1 + 8 * far + x, 8 * y_half : 8 * y_half + 8, :] = value.reshape(3, 8, 128)
+    wrap_rows(v)
+    wide = lax.broadcasted_iota(jnp.int32, (16, 128), 1)
+
+    def one_step(step, carry):
+        section(v, None, a, 0.0, 1.0)
+        section(a, v, b, 0.75, 0.25)
+        section(b, v, v, ONE_THIRD, TWO_THIRDS)
+        return carry
+
+    coarse_ref[...] = jnp.zeros(coarse_ref.shape, jnp.float32)
+
+    def one_snap(k, carry):
+        lax.fori_loop(0, STEPS, one_step, 0)
+        for c in range(3):
+            for block in range(4):
+                at = 1 + 4 * block
+                total = (v[c, at] + v[c, at + 1]) + (v[c, at + 2] + v[c, at + 3])
+                total = total + pltpu.roll(total, 127, 1)
+                total = total + pltpu.roll(total, 126, 1)
+                total = pltpu.roll(total * (1.0 / 16.0), k, 1)
+                coarse_ref[c, block] = jnp.where(wide % 4 == k, total, coarse_ref[c, block])
+        return carry
+
+    lax.fori_loop(0, SNAPS, one_snap, 0)
+    group = lax.broadcasted_iota(jnp.int32, (24, 128), 1) // CHUNK
+    for half in range(2):
+        for far in range(2):
+            for y_half in range(2):
+                value = None
+                for x in range(8):
+                    piece = v[:, 1 + 8 * far + x, 8 * y_half : 8 * y_half + 8, :].reshape(24, 128)
+                    piece = pltpu.roll(piece, (CHUNK * x - 64 * half - HALO) % 128, 1)
+                    value = piece if value is None else jnp.where(group >= x, piece, value)
+                back_ref[2 * (2 * half + far) + y_half] = value.reshape(3, 8, 128)
+
+
+def solve_window(ext):
+    field = pltpu.VMEM((3, 18, 16, 128), jnp.float32)
+    return pl.pallas_call(
+        solve_kernel,
+        out_shape=(
+            jax.ShapeDtypeStruct((GROUP, 3, 8, 128), jnp.float32),
+            jax.ShapeDtypeStruct((3, 4, 16, 128), jnp.float32),
+        ),
+        in_specs=[VMEM_SPEC],
+        out_specs=(VMEM_SPEC, VMEM_SPEC),
+        scratch_shapes=[field, field, field],
+        compiler_params=pltpu.CompilerParams(vmem_limit_bytes=24 * 2**20),
+        name="solve_window",
+    )(ext)
+
+
+def return_kernel(back_ref, coarse_ref, v_ref, pair_ref, landed, send_a, recv_a, send_b, recv_b):
+    gx, gy, gz = lax.axis_index("gx"), lax.axis_index("gy"), lax.axis_index("gz")
+    m = 2 * gx + gy
+    mates = [((m + j) % GROUP) for j in range(1, GROUP)]
+    mate_places = [(k // 2, k % 2, gz) for k in mates]
+    meet(mate_places)
+    partner = (gx, 1 - gy, gz)
+    theirs = pl.multiple_of(8 * (1 - gy), 8)
+    mine = pl.multiple_of(8 * gy, 8)
+    coarse_copy = pltpu.make_async_remote_copy(
+        src_ref=coarse_ref.at[:, :, pl.ds(theirs, 8), :],
+        dst_ref=pair_ref.at[gy],
+        send_sem=send_b,
+        recv_sem=recv_b,
+        device_id=partner,
+        device_id_type=MESH,
+    )
+    coarse_copy.start()
+    copies = []
+    for j in range(1, GROUP):
+        copy = pltpu.make_async_remote_copy(
+            src_ref=back_ref.at[mates[j - 1]],
+            dst_ref=landed.at[m],
+            send_sem=send_a.at[j - 1],
+            recv_sem=recv_a.at[j - 1],
+            device_id=mate_places[j - 1],
+            device_id_type=MESH,
+        )
+        copy.start()
+        copies.append(copy)
+    landed[m] = back_ref[m]
+    pair_ref[gy] = coarse_ref[:, :, pl.ds(mine, 8), :]
+    for copy in copies:
+        copy.wait()
+    rows = swap_groups([landed[k].reshape(24, 128) for k in range(GROUP)])
+    for x in range(8):
+        v_ref[:, x] = rows[x].reshape(3, 8, 128)
+    coarse_copy.wait()
+
+
+def return_blocks(back, coarse):
+    return pl.pallas_call(
+        return_kernel,
+        out_shape=(
+            jax.ShapeDtypeStruct((3, 8, 8, 128), jnp.float32),
+            jax.ShapeDtypeStruct((2, 3, 4, 8, 128), jnp.float32),
+        ),
+        in_specs=[VMEM_SPEC, VMEM_SPEC],
+        out_specs=(VMEM_SPEC, VMEM_SPEC),
+        scratch_shapes=[
+            pltpu.VMEM((GROUP, 3, 8, 128), jnp.float32),
+            pltpu.SemaphoreType.DMA((GROUP - 1,)),
+            pltpu.SemaphoreType.DMA((GROUP - 1,)),
+            pltpu.SemaphoreType.DMA,
+            pltpu.SemaphoreType.DMA,
+        ],
+        compiler_params=pltpu.CompilerParams(
+            collective_id=1, has_side_effects=True, vmem_limit_bytes=16 * 2**20
+        ),
+        name="return_blocks",
+    )(back, coarse)
+
+
+def total_kernel(count_z, part_ref, out_ref, parts, sums, send_a, recv_a, send_b, recv_b, send_c, recv_c):
+    gx, gy, gz = lax.axis_index("gx"), lax.axis_index("gy"), lax.axis_index("gz")
+    m = 2 * gx + gy
+    mates = [((m + j) % GROUP) for j in range(1, GROUP)]
+    mate_places = [(k // 2, k % 2, gz) for k in mates]
+    others = [((gz + j) % count_z) for j in range(1, count_z)]
+    other_places = [(gx, gy, k) for k in others]
+    meet(mate_places + other_places)
+
+    def send(src, dst, send_sem, recv_sem, place):
+        copy = pltpu.make_async_remote_copy(
+            src_ref=src, dst_ref=dst, send_sem=send_sem, recv_sem=recv_sem,
+            device_id=place, device_id_type=MESH,
+        )
+        copy.start()
+        return copy
+
+    copies = [
+        send(part_ref.at[mates[j]], parts.at[m], send_a.at[j], recv_a.at[j], mate_places[j])
+        for j in range(GROUP - 1)
+    ]
+    parts[m] = part_ref[m]
+    for copy in copies:
+        copy.wait()
+    total = parts[0]
+    for k in range(1, GROUP):
+        total = total + parts[k]
+    sums[gz] = total
+    copies = [
+        send(sums.at[gz], sums.at[gz], send_b.at[j], recv_b.at[j], other_places[j])
+        for j in range(count_z - 1)
+    ]
+    for copy in copies:
+        copy.wait()
+    total = sums[0]
+    for k in range(1, count_z):
+        total = total + sums[k]
+    out_ref[m] = total
+    copies = [
+        send(out_ref.at[m], out_ref.at[m], send_c.at[j], recv_c.at[j], mate_places[j])
+        for j in range(GROUP - 1)
+    ]
+    for copy in copies:
+        copy.wait()
+
+
+def total_over_devices(part, count_z):
+    rank = part.shape[0]
+    rows = rank // GROUP
+    sems = pltpu.SemaphoreType.DMA
+    out = pl.pallas_call(
+        functools.partial(total_kernel, count_z),
+        out_shape=jax.ShapeDtypeStruct((GROUP, rows, rank), jnp.float32),
+        in_specs=[VMEM_SPEC],
+        out_specs=VMEM_SPEC,
+        scratch_shapes=[
+            pltpu.VMEM((GROUP, rows, rank), jnp.float32),
+            pltpu.VMEM((count_z, rows, rank), jnp.float32),
+            sems((GROUP - 1,)),
+            sems((GROUP - 1,)),
+            sems((count_z - 1,)),
+            sems((count_z - 1,)),
+            sems((GROUP - 1,)),
+            sems((GROUP - 1,)),
+        ],
+        compiler_params=pltpu.CompilerParams(collective_id=2, has_side_effects=True),
+        name="total_over_devices",
+    )(part.reshape(GROUP, rows, rank))
+    return out.reshape(rank, rank)
+
+
+def omega_of(seed_matrix, snap_steps):
+    picker = (
+        snap_steps[:, None] == jnp.arange(seed_matrix.shape[0], dtype=jnp.int32)[None, :]
+    ).astype(jnp.float32)
+    return 0.5 * jnp.dot(picker, seed_matrix.astype(jnp.float32), precision=HIGHEST)
+
+
+def finish(sketch_rows, gram_sum, rank_keep, shape):
+    rank_total = shape[-1]
+    lower_factor = jnp.linalg.cholesky(gram_sum)
+    identity = jnp.eye(rank_total, dtype=jnp.float32)
+    inverse = lax.linalg.triangular_solve(lower_factor, identity, left_side=True, lower=True).T
+    total_rows = (
+        sketch_rows.shape[0] * lax.axis_size("gx") * lax.axis_size("gy") * lax.axis_size("gz")
+    )
+    norm_scale = math.sqrt(total_rows)
+    inside = (jnp.arange(rank_total, dtype=jnp.int32) < rank_keep[0]).astype(jnp.float32)
+    mode_rows = norm_scale * jnp.dot(sketch_rows, inverse, precision=HIGHEST) * inside[None, :]
+    factor = lower_factor.T * (1.0 / norm_scale) * inside[:, None] * inside[None, :]
+    return mode_rows.reshape(shape), factor
+
+
+def gram_of(sketch_rows):
+    return lax.dot_general(
+        sketch_rows, sketch_rows, (((0,), (0,)), ((), ())), precision=HIGHEST
+    )
+
+
+def by_chunks(velocity, sketch_prev, seed_matrix, snap_steps, rank_keep):
+    rank_total = sketch_prev.shape[-1]
+    count_z = lax.axis_size("gz")
+    ext = gather_blocks(velocity, GROUP * count_z)
+    back, coarse = solve_window(ext)
+    current, pair = return_blocks(back, coarse)
+    omega = omega_of(seed_matrix, snap_steps)
+    spread = pair.reshape(2, 3, 4, 8, 2, 64)[..., HALO : HALO + CHUNK].reshape(2, 3, 4, 8, 2, 4, 4)
+    snap_rows = jnp.transpose(spread, (6, 1, 3, 0, 5, 4, 2)).reshape(SNAPS, -1)
+    sketch_rows = sketch_prev.reshape(-1, rank_total) + lax.dot_general(
+        snap_rows, omega, (((0,), (0,)), ((), ())), precision=HIGHEST
+    )
+    gram_sum = total_over_devices(gram_of(sketch_rows), count_z)
+    return (current,) + finish(sketch_rows, gram_sum, rank_keep, sketch_prev.shape)
+
+
+def step_by_step(velocity, sketch_prev, seed_matrix, snap_steps, rank_keep):
     current = velocity
     collected = []
     for snap_index in range(SNAPS):
@@ -93,28 +473,23 @@
     stacked = jnp.stack(collected)
     rank_total = sketch_prev.shape[-1]
     snap_rows = stacked.reshape(stacked.shape[0], -1)
-    picker = (
-        snap_steps[:, None] == jnp.arange(seed_matrix.shape[0], dtype=jnp.int32)[None, :]
-    ).astype(jnp.float32)
-    omega_rows = 0.5 * jnp.dot(picker, seed_matrix.astype(jnp.float32), precision=HIGHEST)
+    omega_rows = omega_of(seed_matrix, snap_steps)
     sketch_rows = sketch_prev.reshape(-1, rank_total) + lax.dot_general(
         snap_rows, omega_rows, (((0,), (0,)), ((), ())), precision=HIGHEST
     )
-    local_gram = lax.dot_general(
-        sketch_rows, sketch_rows, (((0,), (0,)), ((), ())), precision=HIGHEST
-    )
-    gram_sum = lax.psum(local_gram, ("gx", "gy", "gz"))
-    lower_factor = jnp.linalg.cholesky(gram_sum)
-    identity = jnp.eye(rank_total, dtype=jnp.float32)
-    inverse = lax.linalg.triangular_solve(lower_factor, identity, left_side=True, lower=True).T
-    total_rows = (
-        sketch_rows.shape[0] * lax.axis_size("gx") * lax.axis_size("gy") * lax.axis_size("gz")
-    )
-    norm_scale = math.sqrt(total_rows)
-    inside = (jnp.arange(rank_total, dtype=jnp.int32) < rank_keep[0]).astype(jnp.float32)
-    mode_rows = norm_scale * jnp.dot(sketch_rows, inverse, precision=HIGHEST) * inside[None, :]
-    factor = lower_factor.T * (1.0 / norm_scale) * inside[:, None] * inside[None, :]
-    return (current, mode_rows.reshape(sketch_prev.shape), factor)
+    gram_sum = lax.psum(gram_of(sketch_rows), ("gx", "gy", "gz"))
+    return (current,) + finish(sketch_rows, gram_sum, rank_keep, sketch_prev.shape)
+
+
+def on_device(velocity, sketch_prev, seed_matrix, snap_steps, rank_keep):
+    fits = (
+        (lax.axis_size("gx"), lax.axis_size("gy")) == (4, 2)
+        and lax.axis_size("gz") >= 2
+        and velocity.shape == (3, 8, 8, 128)
+        and sketch_prev.shape == (3, 8, 1, 8, 8, 128)
+    )
+    run = by_chunks if fits else step_by_step
+    return run(velocity, sketch_prev, seed_matrix, snap_steps, rank_keep)
 
 
 def solution(mesh):

time: 684 us -> 94.8 us (0.14); the launches traced: 674 us -> 94.5 us
  waiting for transfers between devices: 370 us -> 0 us
  starting transfers between devices: 217 us -> 0 us
  Pallas kernels: 0 us -> 57.5 us
  other arithmetic: 45.2 us -> 23.8 us
  between operations: 16.8 us -> 1.42 us
  local copies, waits for them, and re-layouts: 19.4 us -> 6.24 us
    ppermute x144 -> x0, waiting for transfers between devices: 241 us -> none  [the longest x72 167 us: extended(): lax.ppermute(lax.slice_in_dim(block, block.shape[dim] - width, None, axis...]
    ppermute x144 -> x0, starting transfers between devices: 201 us -> none  [the longest x72 144 us: extended(): lax.ppermute(lax.slice_in_dim(block, 0, width, axis=dim), axis, backward)]
    psum x1 -> x0, waiting for transfers between devices: 120 us -> none  [on_device(): gram_sum = lax.psum(local_gram, ('gx', 'gy', 'gz'))]
    pallas_call x0 -> x4, Pallas kernels: none -> 57.5 us  [the longest x1 18.6 us: gather_blocks(): pl.pallas_call(functools.partial(gather_kernel, ring), out_shape=jax.Shap...]
    all_to_all x4 -> x0, starting transfers between devices: 14.8 us -> none  [on_device(): lax.all_to_all(local_snap, 'gx', split_axis=2, concat_axis=3, tiled=True)]
    mul x27 -> x2, other arithmetic: 10.3 us -> 0.73 us  [finish(): lower_factor.T * (1.0 / norm_scale) * inside[:, None] * inside[None, :]]
    all_to_all x4 -> x0, waiting for transfers between devices: 9.04 us -> none  [on_device(): lax.all_to_all(local_snap, 'gx', split_axis=2, concat_axis=3, tiled=True)]
  transfers between devices with their start and end apart: 149 -> 0, of which waited for: 121 -> 0; matrix products, arithmetic and copies ran while one was open for 2% -> 0% of each run, Pallas kernels for 0% -> 0%
where the time goes in v1:
time: 94.8 us; the launch traced here: 94.5 us
  Pallas kernels  57.5 us (61%)
  other arithmetic  23.8 us (25%)
  local copies, waits for them, and re-layouts  6.24 us (7%)
  matrix products  5.6 us (6%)
  between operations  1.42 us (1%)
    pallas_call x1, Pallas kernels, gather_blocks(): pl.pallas_call(functools.partial(gather_kernel, ring), out_shape=jax.Shap...  18.6 us
    pallas_call x1, Pallas kernels, solve_window(): pl.pallas_call(solve_kernel, out_shape=(jax.ShapeDtypeStruct((GROUP, 3, 8...  16.1 us
    pallas_call x1, Pallas kernels, total_over_devices(): pl.pallas_call(functools.partial(total_kernel, count_z), out_shape=jax.Sh...  15.5 us
    another operation x3, other arithmetic, finish(): lower_factor = jnp.linalg.cholesky(gram_sum)  12.4 us
    another operation x1, other arithmetic, finish(): lax.linalg.triangular_solve(lower_factor, identity, left_side=True, lower...  9.81 us
    pallas_call x1, Pallas kernels, return_blocks(): pl.pallas_call(return_kernel, out_shape=(jax.ShapeDtypeStruct((3, 8, 8, 1...  7.31 us
    unnamed x10, local copies, waits for them, and re-layouts  2.27 us
    dot_general x1, matrix products, gram_of(): lax.dot_general(sketch_rows, sketch_rows, (((0,), (0,)), ((), ())), preci...  2.05 us

profile of v1, /device:TPU:0, one launch (start us, length us, event | category | flops | bytes accessed | tf_op | source)
XLA Modules:
  0.0 94.5 jit_solution(14246028576977018092)
XLA Ops:
  0.6 0.0 copy-start
  0.6 0.9 copy-done
  1.5 18.6 %gather_blocks.1.ext_ref = f32[5,8,3,8,128]{4,3,2,1,0:T(8,128)S(1)} custom-call(f32[3,8,8,128]{3,2,1,0:T(8,128)S(1)} %copy-done), custom_call_target="tpu_custom_call" | custom-call | tf_op jit(solution)/shard_map/gather_blocks/pallas_call | solution.py:167
  20.1 16.1 %solve_window.1 = (f32[8,3,8,128]{3,2,1,0:T(8,128)S(1)}, f32[3,4,16,128]{3,2,1,0:T(8,128)S(1)}) custom-call(f32[5,8,3,8,128]{4,3,2,1,0:T(8,128)S(1)} %gather_blocks.1.ext_ref), custom_call_target="tpu_custom_call" | custom-call | tf_op jit(solution)/shard_map/solve_window/pallas_call | solution.py:273
  36.2 7.3 %return_blocks.1 = (f32[3,8,8,128]{3,2,1,0:T(8,128)S(1)}, f32[2,3,4,8,128]{4,3,2,1,0:T(8,128)S(1)}) custom-call(f32[8,3,8,128]{3,2,1,0:T(8,128)S(1)} %get-tuple-element.7.back_ref, f32[3,4,16,128]{3,2,1,0:T(8,128)S(1)} %get-tuple-element.8.coarse_ref), custom_call_target="tpu_custom_call" | custom-call | tf_op jit(solution)/shard_map/return_blocks/pallas_call | solution.py:328
  43.5 0.5 copy.17
  44.0 0.0 copy-start.2
  44.0 0.0 copy-start.3
  44.0 0.0 copy-start.1
  44.1 1.5 %copy.13 = f32[4,3,8,2,4,2,4]{6,5,4,3,2,1,0:T(2,128)S(1)} copy(f32[4,3,8,2,4,2,4]{2,0,4,5,6,1,3:T(4,128)S(1)} %bitcast.32) | data formatting | bytes 49152 | tf_op jit(solution)/shard_map/transpose | solution.py:457
  45.6 1.0 %reshape.50 = f32[4,1536]{1,0:T(4,128)S(1)} reshape(f32[4,3,8,2,4,2,4]{6,5,4,3,2,1,0:T(2,128)S(1)} %copy.13) | data formatting | bytes 49152 | tf_op jit(solution)/shard_map/reshape | solution.py:457
  46.6 0.0 copy-done.2
  46.6 0.0 copy-done.3
  46.6 0.2 convolution_multiply_fusion.1
  46.8 0.0 copy-done.1
  46.9 1.4 %convolution_add_fusion = f32[1536,128]{1,0:T(8,128)S(1)} fusion(f32[1536,128]{1,0:T(8,128)S(1)} %bitcast.33, f32[4,1536]{1,0:T(4,128)S(1)} %reshape.50, f32[4,128]{1,0:T(4,128)S(1)} %convolution_multiply_fusion.1), kind=kOutput, calls=%fused_computation.1 | convolution fusion | flops 9633792 | bytes 1599488 | tf_op jit(solution)/shard_map/dot_general | solution.py:458
  48.3 2.0 %fusion.8 = f32[128,128]{1,0:T(8,128)} fusion(f32[1536,128]{1,0:T(8,128)S(1)} %convolution_add_fusion), kind=kOutput, calls=%fused_computation.21 | convolution fusion | flops 301989888 | bytes 851968 | tf_op jit(solution)/shard_map/dot_general | solution.py:444
  50.3 15.5 %total_over_devices.1 = f32[8,16,128]{2,1,0:T(8,128)} custom-call(f32[8,16,128]{2,1,0:T(8,128)} %bitcast.36), custom_call_target="tpu_custom_call" | custom-call | tf_op jit(solution)/shard_map/total_over_devices/pallas_call | solution.py:400
  65.8 0.9 copy.14
  66.8 0.9 fusion.3
  67.6 11.7 %cholesky.17 = f32[128,128]{1,0:T(8,128)S(1)} custom-call(f32[128,128]{1,0:T(8,128)S(1)} %fusion.3), custom_call_target="Cholesky" | custom-call | tf_op jit(solution)/shard_map/jit(cholesky)/cholesky | solution.py:430
  80.0 0.6 compare_reduce_fusion
  80.7 0.7 multiply_bitcast_fusion
  81.4 9.8 %custom-call.6 = f32[1,128,128]{1,2,0:T(8,128)S(1)} custom-call(f32[1,128,128]{2,1,0:T(8,128)S(1)} %get-tuple-element.18), custom_call_target="InvertDiagBlocksLowerTriangular" | custom-call | tf_op jit(solution)/shard_map/triangular_solve | solution.py:432
  91.2 0.2 fusion.1
  91.5 1.7 %convolution_multiply_fusion = f32[1536,128]{1,0:T(8,128)} fusion(f32[1536,128]{1,0:T(8,128)S(1)} %convolution_add_fusion, f32[128,128]{1,0:T(8,128)S(1)} %fusion.1, f32[128]{0:T(128)S(1)} %get-tuple-element.20), kind=kOutput, calls=%fused_computation | convolution fusion | flops 302186496 | bytes 1638912 | tf_op jit(solution)/shard_map/dot_general | solution.py:438
  93.1 0.7 copy.16
  93.9 0.6 copy.20
  (3 shorter events, 0.1 us)
Async XLA Ops:
  0.6 0.9 copy-start
  44.0 2.6 %copy-start.2 = (s32[512,128]{1,0:T(8,128)S(1)}, s32[512,128]{1,0:T(8,128)}, u32[]{:S(2)}) copy-start(s32[512,128]{1,0:T(8,128)} %param.7) | copy-start | bytes 786436
  44.0 2.6 %copy-start.3 = (s32[4]{0:T(128)S(1)}, s32[4]{0:T(128)}, u32[]{:S(2)}) copy-start(s32[4]{0:T(128)} %param.8) | copy-start | bytes 52
  44.0 2.8 %copy-start.1 = (f32[3,8,1,8,8,128]{5,4,3,2,1,0:T(8,128)S(1)}, f32[3,8,1,8,8,128]{5,4,3,2,1,0:T(8,128)}, u32[]{:S(2)}) copy-start(f32[3,8,1,8,8,128]{5,4,3,2,1,0:T(8,128)} %param.6) | copy-start | bytes 2359300

commit v2 on v1

--- a/solution.py
+++ b/solution.py
@@ -425,18 +425,69 @@
     return 0.5 * jnp.dot(picker, seed_matrix.astype(jnp.float32), precision=HIGHEST)
 
 
+def factor_kernel(norm_scale, keep_ref, gram_ref, sketch_ref, rows_ref, factor_ref, unit):
+    rank = gram_ref.shape[0]
+    tiles = rank // 8
+    down = lax.broadcasted_iota(jnp.int32, (8, rank), 0)
+    lane = lax.broadcasted_iota(jnp.int32, (8, rank), 1)
+    left = [gram_ref[8 * t : 8 * t + 8, :] for t in range(tiles)]
+    right = [(lane == down + 8 * t).astype(jnp.float32) for t in range(tiles)]
+
+    def spread(tile, i):
+        return jnp.broadcast_to(tile[i : i + 1, :], (8, rank))
+
+    for k in range(0, rank, 2):
+        home, i = k // 8, k % 8
+        first = [jnp.broadcast_to(left[t][:, k : k + 1], (8, rank)) for t in range(home, tiles)]
+        second = [jnp.broadcast_to(left[t][:, k + 1 : k + 2], (8, rank)) for t in range(home, tiles)]
+        p, q, s = spread(first[0], i), spread(second[0], i), spread(second[0], i + 1)
+        inv_p = 1.0 / p
+        ratio = q * inv_p
+        inv_s = 1.0 / (s - ratio * q)
+        row_a, row_za = spread(left[home], i), spread(right[home], i)
+        row_b = spread(left[home], i + 1) - ratio * row_a
+        row_zb = spread(right[home], i + 1) - ratio * row_za
+        for t in range(home, tiles):
+            m_a = first[t - home] * inv_p
+            m_b = (second[t - home] - first[t - home] * ratio) * inv_s
+            if t == home:
+                m_a = jnp.where(down > i, m_a, 0.0)
+                m_b = jnp.where(down > i + 1, m_b, 0.0)
+            left[t] = left[t] - m_a * row_a - m_b * row_b
+            right[t] = right[t] - m_a * row_za - m_b * row_zb
+    keep = keep_ref[0]
+    for t in range(tiles):
+        at = down + 8 * t
+        pivot = jnp.sum(jnp.where(lane == at, left[t], 0.0), axis=1, keepdims=True)
+        scale = lax.rsqrt(pivot)
+        inside = at < keep
+        factor_ref[8 * t : 8 * t + 8, :] = jnp.where(
+            inside & (lane < keep) & (lane >= at), left[t] * (scale * (1.0 / norm_scale)), 0.0
+        )
+        unit[8 * t : 8 * t + 8, :] = jnp.where(inside, right[t] * (scale * norm_scale), 0.0)
+    rows_ref[...] = lax.dot_general(
+        sketch_ref[...], unit[...], (((1,), (1,)), ((), ())),
+        precision=HIGHEST, preferred_element_type=jnp.float32,
+    )
+
+
 def finish(sketch_rows, gram_sum, rank_keep, shape):
-    rank_total = shape[-1]
-    lower_factor = jnp.linalg.cholesky(gram_sum)
-    identity = jnp.eye(rank_total, dtype=jnp.float32)
-    inverse = lax.linalg.triangular_solve(lower_factor, identity, left_side=True, lower=True).T
+    rank = shape[-1]
     total_rows = (
         sketch_rows.shape[0] * lax.axis_size("gx") * lax.axis_size("gy") * lax.axis_size("gz")
     )
-    norm_scale = math.sqrt(total_rows)
-    inside = (jnp.arange(rank_total, dtype=jnp.int32) < rank_keep[0]).astype(jnp.float32)
-    mode_rows = norm_scale * jnp.dot(sketch_rows, inverse, precision=HIGHEST) * inside[None, :]
-    factor = lower_factor.T * (1.0 / norm_scale) * inside[:, None] * inside[None, :]
+    mode_rows, factor = pl.pallas_call(
+        functools.partial(factor_kernel, math.sqrt(total_rows)),
+        out_shape=(
+            jax.ShapeDtypeStruct(sketch_rows.shape, jnp.float32),
+            jax.ShapeDtypeStruct((rank, rank), jnp.float32),
+        ),
+        in_specs=[pl.BlockSpec(memory_space=pltpu.SMEM), VMEM_SPEC, VMEM_SPEC],
+        out_specs=(VMEM_SPEC, VMEM_SPEC),
+        scratch_shapes=[pltpu.VMEM((rank, rank), jnp.float32)],
+        compiler_params=pltpu.CompilerParams(vmem_limit_bytes=24 * 2**20),
+        name="factor_and_rows",
+    )(rank_keep, gram_sum, sketch_rows)
     return mode_rows.reshape(shape), factor
 
 

time: 94.8 us -> 79.3 us (0.84)
  other arithmetic: 23.8 us -> 0 us
  Pallas kernels: 57.5 us -> 68.8 us
  matrix products: 5.6 us -> 3.68 us
  local copies, waits for them, and re-layouts: 6.24 us -> 5.24 us
    another operation x4 -> x0, other arithmetic: 22.2 us -> none  [the longest x3 12.4 us: finish(): lower_factor = jnp.linalg.cholesky(gram_sum)]
    pallas_call x0 -> x1, Pallas kernels: none -> 11.3 us  [finish(): pl.pallas_call(functools.partial(factor_kernel, math.sqrt(total_rows)), o...]
    dot_general x1 -> x0, matrix products: 1.67 us -> none  [finish(): jnp.dot(sketch_rows, inverse, precision=HIGHEST)]
    unnamed x10 -> x11, local copies, waits for them, and re-layouts: 2.27 us -> 2.38 us
where the time goes in v2:
time: 79.3 us; the launch traced here: 79.1 us
  Pallas kernels  68.8 us (87%)
  local copies, waits for them, and re-layouts  5.24 us (7%)
  matrix products  3.68 us (5%)
  between operations  1.39 us (2%)
    pallas_call x1, Pallas kernels, gather_blocks(): pl.pallas_call(functools.partial(gather_kernel, ring), out_shape=jax.Shap...  18.6 us
    pallas_call x1, Pallas kernels, solve_window(): pl.pallas_call(solve_kernel, out_shape=(jax.ShapeDtypeStruct((GROUP, 3, 8...  16.1 us
    pallas_call x1, Pallas kernels, total_over_devices(): pl.pallas_call(functools.partial(total_kernel, count_z), out_shape=jax.Sh...  15.5 us
    pallas_call x1, Pallas kernels, finish(): pl.pallas_call(functools.partial(factor_kernel, math.sqrt(total_rows)), o...  11.3 us
    pallas_call x1, Pallas kernels, return_blocks(): pl.pallas_call(return_kernel, out_shape=(jax.ShapeDtypeStruct((3, 8, 8, 1...  7.31 us
    unnamed x11, local copies, waits for them, and re-layouts  2.38 us
    dot_general x1, matrix products, gram_of(): lax.dot_general(sketch_rows, sketch_rows, (((0,), (0,)), ((), ())), preci...  2.05 us

profile of v2, /device:TPU:0, one launch (start us, length us, event | category | flops | bytes accessed | tf_op | source)
XLA Modules:
  0.0 79.1 jit_solution(13866544066463931642)
XLA Ops:
  0.6 0.0 copy-start.1
  0.6 0.9 %copy-done.1 = f32[3,8,8,128]{3,2,1,0:T(8,128)S(1)} copy-done((f32[3,8,8,128]{3,2,1,0:T(8,128)S(1)}, f32[3,8,8,128]{3,2,1,0:T(8,128)}, u32[]{:S(2)}) %copy-start.1) | copy-done | bytes 98328
  1.5 18.6 %gather_blocks.1.ext_ref = f32[5,8,3,8,128]{4,3,2,1,0:T(8,128)S(1)} custom-call(f32[3,8,8,128]{3,2,1,0:T(8,128)S(1)} %copy-done.1), custom_call_target="tpu_custom_call" | custom-call | tf_op jit(solution)/shard_map/gather_blocks/pallas_call | solution.py:167
  20.1 16.1 %solve_window.1 = (f32[8,3,8,128]{3,2,1,0:T(8,128)S(1)}, f32[3,4,16,128]{3,2,1,0:T(8,128)S(1)}) custom-call(f32[5,8,3,8,128]{4,3,2,1,0:T(8,128)S(1)} %gather_blocks.1.ext_ref), custom_call_target="tpu_custom_call" | custom-call | tf_op jit(solution)/shard_map/solve_window/pallas_call | solution.py:273
  36.2 7.3 %return_blocks.1 = (f32[3,8,8,128]{3,2,1,0:T(8,128)S(1)}, f32[2,3,4,8,128]{4,3,2,1,0:T(8,128)S(1)}) custom-call(f32[8,3,8,128]{3,2,1,0:T(8,128)S(1)} %get-tuple-element.9.back_ref, f32[3,4,16,128]{3,2,1,0:T(8,128)S(1)} %get-tuple-element.10.coarse_ref), custom_call_target="tpu_custom_call" | custom-call | tf_op jit(solution)/shard_map/return_blocks/pallas_call | solution.py:328
  43.5 0.5 copy.12
  44.0 0.0 copy-start.3
  44.0 0.0 copy-start.4
  44.0 0.0 copy-start.2
  44.1 1.4 %copy.10 = f32[4,3,8,2,4,2,4]{6,5,4,3,2,1,0:T(2,128)S(1)} copy(f32[4,3,8,2,4,2,4]{2,0,4,5,6,1,3:T(4,128)S(1)} %bitcast.16) | data formatting | bytes 49152 | tf_op jit(solution)/shard_map/transpose | solution.py:508
  45.4 1.0 %reshape.31 = f32[4,1536]{1,0:T(4,128)S(1)} reshape(f32[4,3,8,2,4,2,4]{6,5,4,3,2,1,0:T(2,128)S(1)} %copy.10) | data formatting | bytes 49152 | tf_op jit(solution)/shard_map/reshape | solution.py:508
  46.4 0.0 copy-done.3
  46.4 0.0 copy-done.4
  46.5 0.2 convolution_multiply_fusion
  46.7 0.0 copy-done.2
  46.7 1.4 %convolution_add_fusion.sketch_ref = f32[1536,128]{1,0:T(8,128)S(1)} fusion(f32[1536,128]{1,0:T(8,128)S(1)} %bitcast.17, f32[4,1536]{1,0:T(4,128)S(1)} %reshape.31, f32[4,128]{1,0:T(4,128)S(1)} %convolution_multiply_fusion), kind=kOutput, calls=%fused_computation | convolution fusion | flops 9633792 | bytes 1599488 | tf_op jit(solution)/shard_map/dot_general | solution.py:509
  48.1 2.0 %fusion.2 = f32[128,128]{1,0:T(8,128)} fusion(f32[1536,128]{1,0:T(8,128)S(1)} %convolution_add_fusion.sketch_ref), kind=kOutput, calls=%fused_computation.5 | convolution fusion | flops 301989888 | bytes 851968 | tf_op jit(solution)/shard_map/dot_general | solution.py:495
  50.1 15.5 %total_over_devices.1 = f32[8,16,128]{2,1,0:T(8,128)} custom-call(f32[8,16,128]{2,1,0:T(8,128)} %bitcast.18), custom_call_target="tpu_custom_call" | custom-call | tf_op jit(solution)/shard_map/total_over_devices/pallas_call | solution.py:400
  66.3 0.0 copy-start
  66.3 0.8 %copy-done = f32[8,16,128]{2,1,0:T(8,128)S(1)} copy-done((f32[8,16,128]{2,1,0:T(8,128)S(1)}, f32[8,16,128]{2,1,0:T(8,128)}, u32[]{:S(2)}) %copy-start) | copy-done | bytes 65560
  67.1 11.3 %factor_and_rows.1 = (f32[1536,128]{1,0:T(8,128)}, f32[128,128]{1,0:T(8,128)}) custom-call(s32[1]{0:T(128)S(6)} %copy.14.keep_ref, f32[128,128]{1,0:T(8,128)S(1)} %bitcast.14, f32[1536,128]{1,0:T(8,128)S(1)} %convolution_add_fusion.sketch_ref), custom_call_target="tpu_custom_call" | custom-call | tf_op jit(solution)/shard_map/factor_and_rows/pallas_call | solution.py:479
  78.5 0.6 copy.15
  (1 shorter events, 0.0 us)
Async XLA Ops:
  0.6 0.9 %copy-start.1 = (f32[3,8,8,128]{3,2,1,0:T(8,128)S(1)}, f32[3,8,8,128]{3,2,1,0:T(8,128)}, u32[]{:S(2)}) copy-start(f32[3,8,8,128]{3,2,1,0:T(8,128)} %v_ref.1) | copy-start | bytes 294916
  44.0 2.5 %copy-start.3 = (s32[512,128]{1,0:T(8,128)S(1)}, s32[512,128]{1,0:T(8,128)}, u32[]{:S(2)}) copy-start(s32[512,128]{1,0:T(8,128)} %param.7) | copy-start | bytes 786436
  44.0 2.4 %copy-start.4 = (s32[4]{0:T(128)S(1)}, s32[4]{0:T(128)}, u32[]{:S(2)}) copy-start(s32[4]{0:T(128)} %param.8) | copy-start | bytes 52
  44.0 2.7 %copy-start.2 = (f32[3,8,1,8,8,128]{5,4,3,2,1,0:T(8,128)S(1)}, f32[3,8,1,8,8,128]{5,4,3,2,1,0:T(8,128)}, u32[]{:S(2)}) copy-start(f32[3,8,1,8,8,128]{5,4,3,2,1,0:T(8,128)} %param.6) | copy-start | bytes 2359300
  66.3 0.8 %copy-start = (f32[8,16,128]{2,1,0:T(8,128)S(1)}, f32[8,16,128]{2,1,0:T(8,128)}, u32[]{:S(2)}) copy-start(f32[8,16,128]{2,1,0:T(8,128)} %total_over_devices.1) | copy-start | bytes 196612

commit v3 on v2

--- a/solution.py
+++ b/solution.py
@@ -113,11 +113,14 @@
     return rows
 
 
-def meet(places):
+def greet(places):
     barrier = pltpu.get_barrier_semaphore()
     for place in places:
         pl.semaphore_signal(barrier, inc=1, device_id=place, device_id_type=MESH)
-    pl.semaphore_wait(barrier, len(places))
+
+
+def meet(places):
+    pl.semaphore_wait(pltpu.get_barrier_semaphore(), len(places))
 
 
 def gather_kernel(ring, v_ref, ext_ref, packed, send_a, recv_a, send_b, recv_b):
@@ -128,6 +131,7 @@
     mate_places = [(k // 2, k % 2, gz) for k in mates]
     offsets = [d for d in REACH if d != 0]
     ring_places = [place_of((n + d + ring) % ring) for d in offsets]
+    greet(mate_places + ring_places)
     rows = swap_groups([v_ref[:, x].reshape(24, 128) for x in range(8)])
     for k in range(GROUP):
         packed[k] = rows[k].reshape(3, 8, 128)
@@ -289,6 +293,7 @@
     m = 2 * gx + gy
     mates = [((m + j) % GROUP) for j in range(1, GROUP)]
     mate_places = [(k // 2, k % 2, gz) for k in mates]
+    greet(mate_places)
     meet(mate_places)
     partner = (gx, 1 - gy, gz)
     theirs = pl.multiple_of(8 * (1 - gy), 8)
@@ -347,13 +352,15 @@
     )(back, coarse)
 
 
-def total_kernel(count_z, part_ref, out_ref, parts, sums, send_a, recv_a, send_b, recv_b, send_c, recv_c):
+def total_kernel(count_z, sketch_ref, out_ref, part_ref, parts, sums, send_a, recv_a, send_b, recv_b, send_c, recv_c):
     gx, gy, gz = lax.axis_index("gx"), lax.axis_index("gy"), lax.axis_index("gz")
     m = 2 * gx + gy
     mates = [((m + j) % GROUP) for j in range(1, GROUP)]
     mate_places = [(k // 2, k % 2, gz) for k in mates]
     others = [((gz + j) % count_z) for j in range(1, count_z)]
     other_places = [(gx, gy, k) for k in others]
+    greet(mate_places + other_places)
+    part_ref[...] = gram_of(sketch_ref[...]).reshape(part_ref.shape)
     meet(mate_places + other_places)
 
     def send(src, dst, send_sem, recv_sem, place):
@@ -393,8 +400,8 @@
         copy.wait()
 
 
-def total_over_devices(part, count_z):
-    rank = part.shape[0]
+def total_over_devices(sketch_rows, count_z):
+    rank = sketch_rows.shape[1]
     rows = rank // GROUP
     sems = pltpu.SemaphoreType.DMA
     out = pl.pallas_call(
@@ -404,6 +411,7 @@
         out_specs=VMEM_SPEC,
         scratch_shapes=[
             pltpu.VMEM((GROUP, rows, rank), jnp.float32),
+            pltpu.VMEM((GROUP, rows, rank), jnp.float32),
             pltpu.VMEM((count_z, rows, rank), jnp.float32),
             sems((GROUP - 1,)),
             sems((GROUP - 1,)),
@@ -412,9 +420,9 @@
             sems((GROUP - 1,)),
             sems((GROUP - 1,)),
         ],
-        compiler_params=pltpu.CompilerParams(collective_id=2, has_side_effects=True),
+        compiler_params=pltpu.CompilerParams(collective_id=2, has_side_effects=True, vmem_limit_bytes=16 * 2**20),
         name="total_over_devices",
-    )(part.reshape(GROUP, rows, rank))
+    )(sketch_rows)
     return out.reshape(rank, rank)
 
 
@@ -509,7 +517,7 @@
     sketch_rows = sketch_prev.reshape(-1, rank_total) + lax.dot_general(
         snap_rows, omega, (((0,), (0,)), ((), ())), precision=HIGHEST
     )
-    gram_sum = total_over_devices(gram_of(sketch_rows), count_z)
+    gram_sum = total_over_devices(sketch_rows, count_z)
     return (current,) + finish(sketch_rows, gram_sum, rank_keep, sketch_prev.shape)
 
 

time: 79.3 us -> 74.7 us (0.942)
  matrix products: 3.68 us -> 1.63 us
  Pallas kernels: 68.8 us -> 67.1 us
  local copies, waits for them, and re-layouts: 5.24 us -> 4.41 us
    dot_general x1 -> x0, matrix products: 2.05 us -> none  [gram_of(): lax.dot_general(sketch_rows, sketch_rows, (((0,), (0,)), ((), ())), preci...]
    pallas_call x1, Pallas kernels: 15.5 us -> 14.2 us  [total_over_devices(): pl.pallas_call(functools.partial(total_kernel, count_z), out_shape=jax.Sh...]
    unnamed x11 -> x9, local copies, waits for them, and re-layouts: 2.38 us -> 1.55 us
where the time goes in v3:
time: 74.7 us; the launch traced here: 74.5 us
  Pallas kernels  67.1 us (90%)
  local copies, waits for them, and re-layouts  4.41 us (6%)
  matrix products  1.63 us (2%)
  between operations  1.38 us (2%)
    pallas_call x1, Pallas kernels, gather_blocks(): pl.pallas_call(functools.partial(gather_kernel, ring), out_shape=jax.Shap...  18.2 us
    pallas_call x1, Pallas kernels, solve_window(): pl.pallas_call(solve_kernel, out_shape=(jax.ShapeDtypeStruct((GROUP, 3, 8...  16.1 us
    pallas_call x1, Pallas kernels, total_over_devices(): pl.pallas_call(functools.partial(total_kernel, count_z), out_shape=jax.Sh...  14.2 us
    pallas_call x1, Pallas kernels, finish(): pl.pallas_call(functools.partial(factor_kernel, math.sqrt(total_rows)), o...  11.3 us
    pallas_call x1, Pallas kernels, return_blocks(): pl.pallas_call(return_kernel, out_shape=(jax.ShapeDtypeStruct((3, 8, 8, 1...  7.32 us
    unnamed x9, local copies, waits for them, and re-layouts  1.55 us

profile of v3, /device:TPU:0, one launch (start us, length us, event | category | flops | bytes accessed | tf_op | source)
XLA Modules:
  0.0 74.5 jit_solution(14874213684189511654)
XLA Ops:
  0.6 0.0 copy-start
  0.6 0.9 %copy-done = f32[3,8,8,128]{3,2,1,0:T(8,128)S(1)} copy-done((f32[3,8,8,128]{3,2,1,0:T(8,128)S(1)}, f32[3,8,8,128]{3,2,1,0:T(8,128)}, u32[]{:S(2)}) %copy-start) | copy-done | bytes 98328
  1.5 18.2 %gather_blocks.1.ext_ref = f32[5,8,3,8,128]{4,3,2,1,0:T(8,128)S(1)} custom-call(f32[3,8,8,128]{3,2,1,0:T(8,128)S(1)} %copy-done), custom_call_target="tpu_custom_call" | custom-call | tf_op jit(solution)/shard_map/gather_blocks/pallas_call | solution.py:171
  19.8 16.1 %solve_window.1 = (f32[8,3,8,128]{3,2,1,0:T(8,128)S(1)}, f32[3,4,16,128]{3,2,1,0:T(8,128)S(1)}) custom-call(f32[5,8,3,8,128]{4,3,2,1,0:T(8,128)S(1)} %gather_blocks.1.ext_ref), custom_call_target="tpu_custom_call" | custom-call | tf_op jit(solution)/shard_map/solve_window/pallas_call | solution.py:277
  35.9 7.3 %return_blocks.1 = (f32[3,8,8,128]{3,2,1,0:T(8,128)S(1)}, f32[2,3,4,8,128]{4,3,2,1,0:T(8,128)S(1)}) custom-call(f32[8,3,8,128]{3,2,1,0:T(8,128)S(1)} %get-tuple-element.9.back_ref, f32[3,4,16,128]{3,2,1,0:T(8,128)S(1)} %get-tuple-element.10.coarse_ref), custom_call_target="tpu_custom_call" | custom-call | tf_op jit(solution)/shard_map/return_blocks/pallas_call | solution.py:333
  43.2 0.5 copy.12
  43.7 0.0 copy-start.2
  43.7 0.0 copy-start.3
  43.7 0.0 copy-start.1
  43.7 1.4 %copy.10 = f32[4,3,8,2,4,2,4]{6,5,4,3,2,1,0:T(2,128)S(1)} copy(f32[4,3,8,2,4,2,4]{2,0,4,5,6,1,3:T(4,128)S(1)} %bitcast.13) | data formatting | bytes 49152 | tf_op jit(solution)/shard_map/transpose | solution.py:516
  45.1 1.0 %reshape.28 = f32[4,1536]{1,0:T(4,128)S(1)} reshape(f32[4,3,8,2,4,2,4]{6,5,4,3,2,1,0:T(2,128)S(1)} %copy.10) | data formatting | bytes 49152 | tf_op jit(solution)/shard_map/reshape | solution.py:516
  46.1 0.0 copy-done.2
  46.1 0.0 copy-done.3
  46.1 0.2 convolution_multiply_fusion
  46.3 0.0 copy-done.1
  46.3 1.4 %convolution_add_fusion.sketch_ref = f32[1536,128]{1,0:T(8,128)S(1)} fusion(f32[1536,128]{1,0:T(8,128)S(1)} %bitcast.14, f32[4,1536]{1,0:T(4,128)S(1)} %reshape.28, f32[4,128]{1,0:T(4,128)S(1)} %convolution_multiply_fusion), kind=kOutput, calls=%fused_computation | convolution fusion | flops 9633792 | bytes 1599488 | tf_op jit(solution)/shard_map/dot_general | solution.py:517
  47.8 14.2 %total_over_devices.1 = f32[8,16,128]{2,1,0:T(8,128)S(1)} custom-call(f32[1536,128]{1,0:T(8,128)S(1)} %convolution_add_fusion.sketch_ref), custom_call_target="tpu_custom_call" | custom-call | tf_op jit(solution)/shard_map/total_over_devices/pallas_call | solution.py:407
  62.6 11.3 %factor_and_rows.1 = (f32[1536,128]{1,0:T(8,128)}, f32[128,128]{1,0:T(8,128)}) custom-call(s32[1]{0:T(128)S(6)} %copy.14.keep_ref, f32[128,128]{1,0:T(8,128)S(1)} %bitcast.11, f32[1536,128]{1,0:T(8,128)S(1)} %convolution_add_fusion.sketch_ref), custom_call_target="tpu_custom_call" | custom-call | tf_op jit(solution)/shard_map/factor_and_rows/pallas_call | solution.py:487
  73.9 0.6 copy.15
  (1 shorter events, 0.0 us)
Async XLA Ops:
  0.6 0.9 %copy-start = (f32[3,8,8,128]{3,2,1,0:T(8,128)S(1)}, f32[3,8,8,128]{3,2,1,0:T(8,128)}, u32[]{:S(2)}) copy-start(f32[3,8,8,128]{3,2,1,0:T(8,128)} %v_ref.1) | copy-start | bytes 294916
  43.7 2.5 %copy-start.2 = (s32[512,128]{1,0:T(8,128)S(1)}, s32[512,128]{1,0:T(8,128)}, u32[]{:S(2)}) copy-start(s32[512,128]{1,0:T(8,128)} %param.7) | copy-start | bytes 786436
  43.7 2.4 %copy-start.3 = (s32[4]{0:T(128)S(1)}, s32[4]{0:T(128)}, u32[]{:S(2)}) copy-start(s32[4]{0:T(128)} %param.8) | copy-start | bytes 52
  43.7 2.7 %copy-start.1 = (f32[3,8,1,8,8,128]{5,4,3,2,1,0:T(8,128)S(1)}, f32[3,8,1,8,8,128]{5,4,3,2,1,0:T(8,128)}, u32[]{:S(2)}) copy-start(f32[3,8,1,8,8,128]{5,4,3,2,1,0:T(8,128)} %param.6) | copy-start | bytes 2359300

commit v4 on v3

--- a/solution.py
+++ b/solution.py
@@ -215,7 +215,8 @@
             dst[c, r] = (value + x_part) + (y_part + z_part)
         return carry
 
-    lax.fori_loop(1, 17, one_row, 0, unroll=4)
+    for r in range(1, 17):
+        one_row(r, 0)
     wrap_rows(dst)
 
 

time: 74.7 us -> 67.8 us (0.908)
  Pallas kernels: 67.1 us -> 60.3 us
    pallas_call x1, Pallas kernels: 16.1 us -> 9.25 us  [solve_window(): pl.pallas_call(solve_kernel, out_shape=(jax.ShapeDtypeStruct((GROUP, 3, 8...]
where the time goes in v4:
time: 67.8 us; the launch traced here: 67.7 us
  Pallas kernels  60.3 us (89%)
  local copies, waits for them, and re-layouts  4.41 us (7%)
  matrix products  1.63 us (2%)
  between operations  1.38 us (2%)
    pallas_call x1, Pallas kernels, gather_blocks(): pl.pallas_call(functools.partial(gather_kernel, ring), out_shape=jax.Shap...  18.2 us
    pallas_call x1, Pallas kernels, total_over_devices(): pl.pallas_call(functools.partial(total_kernel, count_z), out_shape=jax.Sh...  14.2 us
    pallas_call x1, Pallas kernels, finish(): pl.pallas_call(functools.partial(factor_kernel, math.sqrt(total_rows)), o...  11.3 us
    pallas_call x1, Pallas kernels, solve_window(): pl.pallas_call(solve_kernel, out_shape=(jax.ShapeDtypeStruct((GROUP, 3, 8...  9.25 us
    pallas_call x1, Pallas kernels, return_blocks(): pl.pallas_call(return_kernel, out_shape=(jax.ShapeDtypeStruct((3, 8, 8, 1...  7.32 us
    unnamed x9, local copies, waits for them, and re-layouts  1.55 us
    dot_general x1, matrix products, by_chunks(): lax.dot_general(snap_rows, omega, (((0,), (0,)), ((), ())), precision=HIG...  1.41 us

profile of v4, /device:TPU:0, one launch (start us, length us, event | category | flops | bytes accessed | tf_op | source)
XLA Modules:
  0.0 67.7 jit_solution(14737629362018872140)
XLA Ops:
  0.6 0.0 copy-start
  0.6 0.9 %copy-done = f32[3,8,8,128]{3,2,1,0:T(8,128)S(1)} copy-done((f32[3,8,8,128]{3,2,1,0:T(8,128)S(1)}, f32[3,8,8,128]{3,2,1,0:T(8,128)}, u32[]{:S(2)}) %copy-start) | copy-done | bytes 98328
  1.5 18.2 %gather_blocks.1.ext_ref = f32[5,8,3,8,128]{4,3,2,1,0:T(8,128)S(1)} custom-call(f32[3,8,8,128]{3,2,1,0:T(8,128)S(1)} %copy-done), custom_call_target="tpu_custom_call" | custom-call | tf_op jit(solution)/shard_map/gather_blocks/pallas_call | solution.py:171
  19.8 9.2 %solve_window.1 = (f32[8,3,8,128]{3,2,1,0:T(8,128)S(1)}, f32[3,4,16,128]{3,2,1,0:T(8,128)S(1)}) custom-call(f32[5,8,3,8,128]{4,3,2,1,0:T(8,128)S(1)} %gather_blocks.1.ext_ref), custom_call_target="tpu_custom_call" | custom-call | tf_op jit(solution)/shard_map/solve_window/pallas_call | solution.py:278
  29.0 7.3 %return_blocks.1 = (f32[3,8,8,128]{3,2,1,0:T(8,128)S(1)}, f32[2,3,4,8,128]{4,3,2,1,0:T(8,128)S(1)}) custom-call(f32[8,3,8,128]{3,2,1,0:T(8,128)S(1)} %get-tuple-element.9.back_ref, f32[3,4,16,128]{3,2,1,0:T(8,128)S(1)} %get-tuple-element.10.coarse_ref), custom_call_target="tpu_custom_call" | custom-call | tf_op jit(solution)/shard_map/return_blocks/pallas_call | solution.py:334
  36.3 0.5 copy.12
  36.8 0.0 copy-start.2
  36.8 0.0 copy-start.3
  36.8 0.0 copy-start.1
  36.9 1.4 %copy.10 = f32[4,3,8,2,4,2,4]{6,5,4,3,2,1,0:T(2,128)S(1)} copy(f32[4,3,8,2,4,2,4]{2,0,4,5,6,1,3:T(4,128)S(1)} %bitcast.13) | data formatting | bytes 49152 | tf_op jit(solution)/shard_map/transpose | solution.py:517
  38.3 1.0 %reshape.28 = f32[4,1536]{1,0:T(4,128)S(1)} reshape(f32[4,3,8,2,4,2,4]{6,5,4,3,2,1,0:T(2,128)S(1)} %copy.10) | data formatting | bytes 49152 | tf_op jit(solution)/shard_map/reshape | solution.py:517
  39.3 0.0 copy-done.2
  39.3 0.0 copy-done.3
  39.3 0.2 convolution_multiply_fusion
  39.5 0.0 copy-done.1
  39.5 1.4 %convolution_add_fusion.sketch_ref = f32[1536,128]{1,0:T(8,128)S(1)} fusion(f32[1536,128]{1,0:T(8,128)S(1)} %bitcast.14, f32[4,1536]{1,0:T(4,128)S(1)} %reshape.28, f32[4,128]{1,0:T(4,128)S(1)} %convolution_multiply_fusion), kind=kOutput, calls=%fused_computation | convolution fusion | flops 9633792 | bytes 1599488 | tf_op jit(solution)/shard_map/dot_general | solution.py:518
  40.9 14.2 %total_over_devices.1 = f32[8,16,128]{2,1,0:T(8,128)S(1)} custom-call(f32[1536,128]{1,0:T(8,128)S(1)} %convolution_add_fusion.sketch_ref), custom_call_target="tpu_custom_call" | custom-call | tf_op jit(solution)/shard_map/total_over_devices/pallas_call | solution.py:408
  55.7 11.3 %factor_and_rows.1 = (f32[1536,128]{1,0:T(8,128)}, f32[128,128]{1,0:T(8,128)}) custom-call(s32[1]{0:T(128)S(6)} %copy.14.keep_ref, f32[128,128]{1,0:T(8,128)S(1)} %bitcast.11, f32[1536,128]{1,0:T(8,128)S(1)} %convolution_add_fusion.sketch_ref), custom_call_target="tpu_custom_call" | custom-call | tf_op jit(solution)/shard_map/factor_and_rows/pallas_call | solution.py:488
  67.0 0.6 copy.15
  (1 shorter events, 0.0 us)
Async XLA Ops:
  0.6 0.9 %copy-start = (f32[3,8,8,128]{3,2,1,0:T(8,128)S(1)}, f32[3,8,8,128]{3,2,1,0:T(8,128)}, u32[]{:S(2)}) copy-start(f32[3,8,8,128]{3,2,1,0:T(8,128)} %v_ref.1) | copy-start | bytes 294916
  36.8 2.5 %copy-start.2 = (s32[512,128]{1,0:T(8,128)S(1)}, s32[512,128]{1,0:T(8,128)}, u32[]{:S(2)}) copy-start(s32[512,128]{1,0:T(8,128)} %param.7) | copy-start | bytes 786436
  36.8 2.4 %copy-start.3 = (s32[4]{0:T(128)S(1)}, s32[4]{0:T(128)}, u32[]{:S(2)}) copy-start(s32[4]{0:T(128)} %param.8) | copy-start | bytes 52
  36.8 2.7 %copy-start.1 = (f32[3,8,1,8,8,128]{5,4,3,2,1,0:T(8,128)S(1)}, f32[3,8,1,8,8,128]{5,4,3,2,1,0:T(8,128)}, u32[]{:S(2)}) copy-start(f32[3,8,1,8,8,128]{5,4,3,2,1,0:T(8,128)} %param.6) | copy-start | bytes 2359300
